TPU v7x, 32 devices: a whole 2x2x4 slice. The times are simulated.
32 devices in a mesh: px: 4 (over z), py: 2 (over x), dz: 4 (over y, core).
Axes of the slice: x: 2, y: 2, z: 4, core: 2. Of those that a mesh axis runs over, the one named last changes fastest.
Arguments:
- near_state: float32 [3, 32, 192, 512], P(None, 'px', 'dz', 'py'), may hold values from -1 to 1, as said below
- column_owner: int32 [4, 8, 512, 1], P('px', ('py', 'dz')), may hold values from 0 to 7; in each aligned block of 512 rows (0 to 511, 512 to 1023, ..., all dimensions but the last counted through in order) at most 128 rows name the same one
- landing: int32 [4, 8, 512], P('px', ('py', 'dz')), may hold values from 0 to 16383
- far_depth: float32 [256, 2048], P('px', ('py', 'dz')), may hold values from 3 to 6
- far_flows: float32 [2, 256, 2048], P(None, 'px', ('py', 'dz')), may hold values from -3 to 3
- wet_mask: int32 [256, 2048], P('px', ('py', 'dz')), may hold values 0 or 1
Outputs:
- near_fraction: float32 [32, 192, 512], P('px', 'dz', 'py')
- far_new: float32 [3, 256, 2048], P(None, 'px', ('py', 'dz'))
Inputs may be any that keep to these rules, and one draw needn't show every extreme that they name: `near_state`: the volume fraction (first field) lies in 0 to 1; the velocities lie in -1 to 1. `column_owner`: in each near tile no owner receives more than 128 columns; some owner receives exactly 128.
All inputs are finite; a program needn't handle non-finite values. No bound on the sum of `wet_mask` on one device may be relied on, other than what follows from the above.
Results may differ from a plain program's by a relative error of at most 0.00002.
Values sent between devices are 32-bit elements; how exact they have to be, the bound alone decides.
A program may use at most 64 MiB of HBM per device.

v0:
```python
import jax
import jax.numpy as jnp
from jax import lax
from jax.sharding import PartitionSpec as P

CAP = 128


advect_coef = 0.25
diffuse_coef = 0.1
slope_coef = 0.5
flux_coef = 0.1
gravity = 1.0
column_height = 4.0


def padded_2(cells, sides, width):
    for axis, dim in sides:
        count = lax.axis_size(axis)
        ends = count - 1
        head = lax.slice_in_dim(cells, 0, width, axis=dim)
        tail = lax.slice_in_dim(cells, cells.shape[dim] - width, cells.shape[dim], axis=dim)
        cells = jnp.concatenate(
            [
                lax.ppermute(tail, axis, [(i, (i + 1) % count) for i in range(ends)]),
                cells,
                lax.ppermute(head, axis, [((i + 1) % count, i) for i in range(ends)]),
            ],
            axis=dim,
        )
    return cells


def near_update(center, xplus, xminus, yplus, yminus, zplus, zminus):
    velx = center[1]
    vely = center[2]
    lap = xplus + xminus + yplus + yminus + zplus + zminus - 6.0 * center
    moved = (
        center
        - advect_coef * (velx * (xplus - xminus) + vely * (yplus - yminus))
        + diffuse_coef * lap
    )
    new_frac = moved[0]
    new_velx = moved[1] - slope_coef * (xplus[0] - xminus[0])
    new_vely = moved[2] - slope_coef * (yplus[0] - yminus[0])
    return (new_frac, new_velx, new_vely)


def fluxes(state, divisor):
    depth = state[0]
    flow_x = state[1]
    flow_y = state[2]
    cross = flow_x * flow_y / divisor
    press = 0.5 * gravity * depth * depth
    xflux = jnp.stack([flow_x, flow_x * flow_x / divisor + press, cross])
    yflux = jnp.stack([flow_y, cross, flow_y * flow_y / divisor + press])
    return (xflux, yflux)


def local(near_state, column_owner, landing, far_depth, far_flows, wet_mask):
    padded = padded_2(near_state, (("px", 1), ("py", 3), ("dz", 2)), 1)
    center = padded[:, 1:-1, 1:-1, 1:-1]
    new_frac, new_velx, new_vely = near_update(
        center,
        padded[:, 2:, 1:-1, 1:-1],
        padded[:, :-2, 1:-1, 1:-1],
        padded[:, 1:-1, 1:-1, 2:],
        padded[:, 1:-1, 1:-1, :-2],
        padded[:, 1:-1, 2:, 1:-1],
        padded[:, 1:-1, :-2, 1:-1],
    )
    inv_depth = column_height / (near_state.shape[2] * lax.axis_size("dz"))
    partial_sums = jnp.stack(
        [
            jnp.sum(new_frac, axis=1),
            jnp.sum(new_frac * new_velx, axis=1),
            jnp.sum(new_frac * new_vely, axis=1),
        ]
    )
    columns = lax.psum_scatter(partial_sums, "dz", scatter_dimension=2, tiled=True) * inv_depth
    count_cols = columns.shape[1] * columns.shape[2]
    columns = columns.reshape(3, count_cols)
    owners = lax.axis_size("py") * lax.axis_size("dz")
    capacity = CAP
    dest = column_owner[0, 0, :, 0]
    land = landing[0, 0, :]
    onehot = (dest[:, None] == jnp.arange(owners, dtype=jnp.int32)[None, :]).astype(jnp.int32)
    rank = jnp.sum(jnp.cumsum(onehot, axis=0) * onehot, axis=1) - 1
    slot = dest * capacity + rank
    packed = jnp.concatenate([columns, land.astype(jnp.float32)[None, :]], axis=0)
    blank = jnp.concatenate(
        [
            jnp.zeros((3, owners * capacity), jnp.float32),
            jnp.full((1, owners * capacity), -1.0, jnp.float32),
        ],
        axis=0,
    )
    buffer = blank.at[:, slot].set(packed)
    arrived = lax.all_to_all(
        buffer.reshape(4, owners, capacity), ("py", "dz"), split_axis=1, concat_axis=1, tiled=True
    )
    arrived = arrived.reshape(4, owners * capacity)
    far_x = far_depth.shape[0]
    far_y = far_depth.shape[1]
    valid = arrived[3] >= 0.0
    target = jnp.where(valid, arrived[3], 0.0).astype(jnp.int32)
    values = jnp.where(valid[None, :], arrived[0:3], 0.0)
    source = (
        jnp.zeros((3, far_x * far_y), jnp.float32)
        .at[:, target]
        .add(values)
        .reshape(3, far_x, far_y)
    )
    wet = wet_mask.astype(jnp.float32)
    state = jnp.stack([far_depth, far_flows[0], far_flows[1]]) + source
    state = jnp.stack([state[0], state[1] * wet, state[2] * wet])
    state_pad = padded_2(state, (("px", 1), (("py", "dz"), 2)), 1)
    row_global = jnp.arange(far_x + 2, dtype=jnp.int32) + lax.axis_index("px") * far_x - 1
    col_global = jnp.arange(far_y + 2, dtype=jnp.int32) + lax.axis_index(("py", "dz")) * far_y - 1
    row_inside = (row_global >= 0) & (row_global < far_x * lax.axis_size("px"))
    col_inside = (col_global >= 0) & (col_global < far_y * lax.axis_size(("py", "dz")))
    inside = row_inside[:, None] & col_inside[None, :]
    divisor = jnp.where(inside, state_pad[0], 1.0)
    xpad, ypad = fluxes(state_pad, divisor)
    avg = 0.25 * (
        state_pad[:, 2:, 1:-1]
        + state_pad[:, :-2, 1:-1]
        + state_pad[:, 1:-1, 2:]
        + state_pad[:, 1:-1, :-2]
    )
    far_new = (
        avg
        - flux_coef * (xpad[:, 2:, 1:-1] - xpad[:, :-2, 1:-1])
        - flux_coef * (ypad[:, 1:-1, 2:] - ypad[:, 1:-1, :-2])
    )
    return (new_frac, far_new)


def solution(mesh):
    return jax.shard_map(
        local,
        mesh=mesh,
        in_specs=(
            P(None, "px", "dz", "py"),
            P("px", ("py", "dz"), None, None),
            P("px", ("py", "dz"), None),
            P("px", ("py", "dz")),
            P(None, "px", ("py", "dz")),
            P("px", ("py", "dz")),
        ),
        out_specs=(P("px", "dz", "py"), P(None, "px", ("py", "dz"))),
        check_vma=False,
    )
```

profile of v0, /device:TPU:1, one launch (start us, length us, event | category | flops | bytes accessed | tf_op | source)
XLA Modules:
  0.0 115.4 jit_solution(14838108347821971654)
XLA Ops:
  7.2 1.0 fusion.41
  8.2 4.2 %collective-permute-start.1 = (f32[3,1,48,256]{3,2,1,0:T(8,128)S(1)}, f32[3,1,48,256]{3,2,1,0:T(8,128)S(1)}, u32[]{:S(2)}, u32[]{:S(2)}) collective-permute-start(f32[3,1,48,256]{3,2,1,0:T(8,128)S(1)} %get-tuple-element.19), channel_id=1, source_target_pairs={{0,8},{8,16},{16,24},{1,9},{9,17},{17,25},{2,10},{10,18},{18,26},{... | collective-permute-start | bytes 442376 | tf_op jit(solution)/shard_map/ppermute | solution.py:25
  12.4 1.3 %collective-permute-start = (f32[3,1,48,256]{3,2,1,0:T(8,128)S(1)}, f32[3,1,48,256]{3,2,1,0:T(8,128)S(1)}, u32[]{:S(2)}, u32[]{:S(2)}) collective-permute-start(f32[3,1,48,256]{3,2,1,0:T(8,128)S(1)} %get-tuple-element.18), channel_id=1, source_target_pairs={{8,0},{16,8},{24,16},{9,1},{17,9},{25,17},{10,2},{18,10},{26,18},{... | collective-permute-start | bytes 442376 | tf_op jit(solution)/shard_map/ppermute | solution.py:27
  13.7 1.9 %slice_bitcast_fusion.1 = (f32[8,48,256]{2,1,0:T(8,128)S(1)}, f32[8,48,256]{2,1,0:T(8,128)}) fusion(f32[3,8,48,256]{3,2,1,0:T(8,128)} %param.6), kind=kLoop, calls=%fused_computation.36 | loop fusion | bytes 1572864 | tf_op jit(solution)/shard_map/mul | solution.py:40
  15.6 1.1 reduce-window.6
  17.2 0.3 constant_dynamic-update-slice_fusion.5
  17.5 1.2 %collective-permute-done = f32[3,1,48,256]{3,2,1,0:T(8,128)S(1)} collective-permute-done((f32[3,1,48,256]{3,2,1,0:T(8,128)S(1)}, f32[3,1,48,256]{3,2,1,0:T(8,128)S(1)}, u32[]{:S(2)}, u32[]{:S(2)}) %collective-permute-start) | collective-permute-done | bytes 147488 | tf_op jit(solution)/shard_map/ppermute | solution.py:27
  19.0 0.8 copy-done.2
  20.1 1.3 %collective-permute-start.2 = (f32[3,10,48,1]{2,3,1,0:T(1,128)S(1)}, f32[3,10,48,1]{2,3,1,0:T(1,128)S(1)}, u32[]{:S(2)}, u32[]{:S(2)}) collective-permute-start(f32[3,10,48,1]{2,3,1,0:T(1,128)S(1)} %copy.56), channel_id=1, source_target_pairs={{4,0},{5,1},{6,2},{7,3},{12,8},{13,9},{14,10},{15,11},{20,16},{21,... | collective-permute-start | bytes 17288 | tf_op jit(solution)/shard_map/ppermute | solution.py:27
  21.7 4.0 %collective-permute-start.3 = (f32[3,10,48,1]{2,3,1,0:T(1,128)S(1)}, f32[3,10,48,1]{2,3,1,0:T(1,128)S(1)}, u32[]{:S(2)}, u32[]{:S(2)}) collective-permute-start(f32[3,10,48,1]{2,3,1,0:T(1,128)S(1)} %copy.57), channel_id=1, source_target_pairs={{0,4},{1,5},{2,6},{3,7},{8,12},{9,13},{10,14},{11,15},{16,20},{17,... | collective-permute-start | bytes 17288 | tf_op jit(solution)/shard_map/ppermute | solution.py:25
  26.0 0.5 collective-permute-done.3
  27.2 6.2 %collective-permute-start.5 = (f32[3,10,1,258]{3,2,1,0:T(1,128)S(1)}, f32[3,10,1,258]{3,2,1,0:T(1,128)S(1)}, u32[]{:S(2)}, u32[]{:S(2)}) collective-permute-start(f32[3,10,1,258]{3,2,1,0:T(1,128)S(1)} %get-tuple-element.10), channel_id=1, source_target_pairs={{0,1},{1,2},{2,3},{4,5},{5,6},{6,7},{8,9},{9,10},{10,11},{12,13},{... | collective-permute-start | bytes 92888 | tf_op jit(solution)/shard_map/ppermute | solution.py:25
  33.4 1.9 %collective-permute-start.4 = (f32[3,10,1,258]{3,2,1,0:T(1,128)S(1)}, f32[3,10,1,258]{3,2,1,0:T(1,128)S(1)}, u32[]{:S(2)}, u32[]{:S(2)}) collective-permute-start(f32[3,10,1,258]{3,2,1,0:T(1,128)S(1)} %get-tuple-element.9), channel_id=1, source_target_pairs={{1,0},{2,1},{3,2},{5,4},{6,5},{7,6},{9,8},{10,9},{11,10},{13,12},{... | collective-permute-start | bytes 92888 | tf_op jit(solution)/shard_map/ppermute | solution.py:27
  35.3 3.4 %collective-permute-done.4 = f32[3,10,1,258]{3,2,1,0:T(1,128)S(1)} collective-permute-done((f32[3,10,1,258]{3,2,1,0:T(1,128)S(1)}, f32[3,10,1,258]{3,2,1,0:T(1,128)S(1)}, u32[]{:S(2)}, u32[]{:S(2)}) %collective-permute-start.4) | collective-permute-done | bytes 30992 | tf_op jit(solution)/shard_map/ppermute | solution.py:27
  38.8 3.5 %fusion.7 = f32[3,8,48,256]{3,2,1,0:T(8,128)S(1)} fusion(f32[3,10,1,258]{3,2,1,0:T(1,128)S(1)} %collective-permute-done.5, f32[3,10,48,1]{3,2,1,0:T(8,128)S(1)} %copy.44, f32[3,10,48,256]{3,2,1,0:T(8,128)S(1)} %get-tuple-element.31, f32[3,10,48,1]{3,2,1,0:T(8,128)S(1)} %copy.46, f32[3,10,1,258]{3,2,1,0:T(1,128)S(1)} %collective-permute-done.4, ...), kind=kLoop, calls=%fused_computation.14 | loop fusion | flops 7077888 | bytes 7053024 | tf_op jit(solution)/shard_map/add | solution.py:39
  42.3 2.1 %fusion.19 = (f32[8,256]{1,0:T(8,128)S(1)}, f32[8,256]{1,0:T(8,128)S(1)}, f32[8,48,256]{2,1,0:T(8,128)}) fusion(f32[3,9,48,256]{3,2,1,0:T(8,128)} %copy-done.5, f32[3,9,48,256]{3,2,1,0:T(8,128)S(1)} %copy-done.3, f32[3,8,48,256]{3,2,1,0:T(8,128)S(1)} %fusion.7, f32[3,10,48,256]{3,2,1,0:T(8,128)S(1)} %get-tuple-element.31, f32[3,10,48,1]{3,2,1,0:T(8,128)S(1)} %copy.46, ...), kind=kLoop, calls=%fused_computation.34 | loop fusion | flops 1175552 | bytes 3861760 | tf_op jit(solution)/shard_map/reduce_sum | solution.py:76
  44.7 0.9 reshape.229
  45.6 19.2 %reduce-scatter.4.cloned.1.call-done = f32[64,24]{1,0:T(8,128)} async-done(((f32[256,24]{1,0:T(8,128)}), f32[64,24]{1,0:T(8,128)}) %reduce-scatter.4.cloned.1.call-update) | async-done | bytes 6160
  64.8 0.9 reshape.230
  66.0 1.9 %scatter_fusion = f32[4,1024]{0,1:T(8,128)S(1)} fusion(f32[4,1024]{0,1:T(8,128)S(1)} %copy-done.4, s32[512]{0:T(512)S(1)} %bitcast.87, f32[512,4]{1,0:T(8,128)S(1)} %copy.49), kind=kCustom, calls=%fused_computation | custom fusion | bytes 26624 | tf_op jit(solution)/shard_map/scatter | solution.py:98
  68.0 0.8 copy.50
  68.8 4.4 %all-to-all-start = ((f32[4,8,128]{2,0,1:T(4,128)}), f32[4,8,128]{2,0,1:T(4,128)S(1)}, u32[]{:S(2)}, u32[]{:S(2)}) async-start(f32[4,8,128]{2,0,1:T(4,128)} %copy.50), calls=%async_computation | async-start | bytes 32768 | tf_op jit(solution)/shard_map/all_to_all | solution.py:99
  73.2 4.0 %all-to-all-done = f32[4,8,128]{2,0,1:T(4,128)S(1)} async-done(((f32[4,8,128]{2,0,1:T(4,128)}), f32[4,8,128]{2,0,1:T(4,128)S(1)}, u32[]{:S(2)}, u32[]{:S(2)}) %all-to-all-start) | async-done | bytes 16416 | tf_op jit(solution)/shard_map/all_to_all | solution.py:99
  77.5 10.6 %scatter_custom_fusion.1 = f32[3,16384]{0,1:T(8,128)} fusion(s32[1024]{0:T(1024)S(1)} %bitcast.89, f32[1024,3]{1,0:T(8,128)S(1)} %copy.52, f32[]{:T(128)} %constant.23.clone.1), kind=kCustom, calls=%fused_computation.2 | custom fusion | flops 3072 | bytes 196612 | tf_op jit(solution)/shard_map/scatter-add | solution.py:111
  88.1 5.3 %copy.53 = f32[3,64,256]{2,1,0:T(8,128)S(1)} copy(f32[3,64,256]{0,2,1:T(8,128)} %bitcast.76) | data formatting | bytes 393216 | tf_op jit(solution)/shard_map/reshape | solution.py:112
  93.4 1.3 %collective-permute-start.6 = (f32[3,1,256]{2,1,0:T(1,128)S(1)}, f32[3,1,256]{2,1,0:T(1,128)S(1)}, u32[]{:S(2)}, u32[]{:S(2)}) collective-permute-start(f32[3,1,256]{2,1,0:T(1,128)S(1)} %get-tuple-element.30), channel_id=1, source_target_pairs={{8,0},{16,8},{24,16},{9,1},{17,9},{25,17},{10,2},{18,10},{26,18},{... | collective-permute-start | bytes 9224 | tf_op jit(solution)/shard_map/ppermute | solution.py:27
  94.7 4.0 %collective-permute-start.7 = (f32[3,1,256]{2,1,0:T(1,128)S(1)}, f32[3,1,256]{2,1,0:T(1,128)S(1)}, u32[]{:S(2)}, u32[]{:S(2)}) collective-permute-start(f32[3,1,256]{2,1,0:T(1,128)S(1)} %get-tuple-element.29), channel_id=1, source_target_pairs={{0,8},{8,16},{16,24},{1,9},{9,17},{17,25},{2,10},{10,18},{18,26},{... | collective-permute-start | bytes 9224 | tf_op jit(solution)/shard_map/ppermute | solution.py:25
  98.8 0.7 collective-permute-done.7
  99.6 3.9 %collective-permute-start.8 = (f32[3,66,1]{2,1,0:T(8,128)S(1)}, f32[3,66,1]{2,1,0:T(8,128)S(1)}, u32[]{:S(2)}, u32[]{:S(2)}) collective-permute-start(f32[3,66,1]{2,1,0:T(8,128)S(1)} %get-tuple-element.28), channel_id=1, source_target_pairs={{1,0},{2,1},{3,2},{4,3},{5,4},{6,5},{7,6},{9,8},{10,9},{11,10},{12... | collective-permute-start | bytes 2384 | tf_op jit(solution)/shard_map/ppermute | solution.py:27
  103.5 1.9 %collective-permute-start.9 = (f32[3,66,1]{2,1,0:T(8,128)S(1)}, f32[3,66,1]{2,1,0:T(8,128)S(1)}, u32[]{:S(2)}, u32[]{:S(2)}) collective-permute-start(f32[3,66,1]{2,1,0:T(8,128)S(1)} %get-tuple-element.27), channel_id=1, source_target_pairs={{0,1},{1,2},{2,3},{3,4},{4,5},{5,6},{6,7},{8,9},{9,10},{10,11},{11... | collective-permute-start | bytes 2384 | tf_op jit(solution)/shard_map/ppermute | solution.py:25
  105.6 1.5 %collective-permute-done.9 = f32[3,66,1]{2,1,0:T(8,128)S(1)} collective-permute-done((f32[3,66,1]{2,1,0:T(8,128)S(1)}, f32[3,66,1]{2,1,0:T(8,128)S(1)}, u32[]{:S(2)}, u32[]{:S(2)}) %collective-permute-start.9) | collective-permute-done | bytes 824 | tf_op jit(solution)/shard_map/ppermute | solution.py:25
  107.5 1.1 fusion.21
  (70 shorter events, 4.0 us)
Async XLA Ops:
  7.2 8.5 %copy-start.10 = (s32[1,1,512,1]{2,3,1,0:T(1,128)S(1)}, s32[1,1,512,1]{2,3,1,0:T(1,128)}, u32[]{:S(2)}) copy-start(s32[1,1,512,1]{2,3,1,0:T(1,128)} %param.7) | copy-start | bytes 6148
  7.2 57.6 %reduce-scatter.4.cloned.1.call-start = ((), (), s32[]{:S(2)}) async-start(), calls=%async_computation.2 | async-start | bytes 163840
  8.2 9.0 %copy-start = (f32[3,8,48,256]{3,2,1,0:T(8,128)S(1)}, f32[3,8,48,256]{3,2,1,0:T(8,128)}, u32[]{:S(2)}) copy-start(f32[3,8,48,256]{3,2,1,0:T(8,128)} %param.6) | copy-start | bytes 3538948
  8.2 8.9 %collective-permute-start.1 = (f32[3,1,48,256]{3,2,1,0:T(8,128)S(1)}, f32[3,1,48,256]{3,2,1,0:T(8,128)S(1)}, u32[]{:S(2)}, u32[]{:S(2)}) collective-permute-start(f32[3,1,48,256]{3,2,1,0:T(8,128)S(1)} %get-tuple-element.19), channel_id=1, source_target_pairs={{0,8},{8,16},{16,24},{1,9},{9,17},{17,25},{2,10},{10,18},{18,26},{... | collective-permute-start | bytes 442376 | tf_op jit(solution)/shard_map/ppermute | solution.py:25
  12.4 6.3 %collective-permute-start = (f32[3,1,48,256]{3,2,1,0:T(8,128)S(1)}, f32[3,1,48,256]{3,2,1,0:T(8,128)S(1)}, u32[]{:S(2)}, u32[]{:S(2)}) collective-permute-start(f32[3,1,48,256]{3,2,1,0:T(8,128)S(1)} %get-tuple-element.18), channel_id=1, source_target_pairs={{8,0},{16,8},{24,16},{9,1},{17,9},{25,17},{10,2},{18,10},{26,18},{... | collective-permute-start | bytes 442376 | tf_op jit(solution)/shard_map/ppermute | solution.py:27
  17.5 1.5 %copy-start.5 = (f32[3,9,48,256]{3,2,1,0:T(8,128)}, f32[3,9,48,256]{3,2,1,0:T(8,128)S(1)}, u32[]{:S(2)}) copy-start(f32[3,9,48,256]{3,2,1,0:T(8,128)S(1)} %get-tuple-element.16) | copy-start | bytes 3981316
  18.7 1.1 copy-start.2
  20.1 5.6 %collective-permute-start.2 = (f32[3,10,48,1]{2,3,1,0:T(1,128)S(1)}, f32[3,10,48,1]{2,3,1,0:T(1,128)S(1)}, u32[]{:S(2)}, u32[]{:S(2)}) collective-permute-start(f32[3,10,48,1]{2,3,1,0:T(1,128)S(1)} %copy.56), channel_id=1, source_target_pairs={{4,0},{5,1},{6,2},{7,3},{12,8},{13,9},{14,10},{15,11},{20,16},{21,... | collective-permute-start | bytes 17288 | tf_op jit(solution)/shard_map/ppermute | solution.py:27
  21.7 4.8 %collective-permute-start.3 = (f32[3,10,48,1]{2,3,1,0:T(1,128)S(1)}, f32[3,10,48,1]{2,3,1,0:T(1,128)S(1)}, u32[]{:S(2)}, u32[]{:S(2)}) collective-permute-start(f32[3,10,48,1]{2,3,1,0:T(1,128)S(1)} %copy.57), channel_id=1, source_target_pairs={{0,4},{1,5},{2,6},{3,7},{8,12},{9,13},{10,14},{11,15},{16,20},{17,... | collective-permute-start | bytes 17288 | tf_op jit(solution)/shard_map/ppermute | solution.py:25
  26.8 11.9 %copy-start.1 = (f32[3,8,48,256]{3,2,1,0:T(8,128)S(1)}, f32[3,8,48,256]{3,2,1,0:T(8,128)}, u32[]{:S(2)}) copy-start(f32[3,8,48,256]{3,2,1,0:T(8,128)} %param.6) | copy-start | bytes 3538948
  26.8 11.9 %copy-start.3 = (f32[3,9,48,256]{3,2,1,0:T(8,128)S(1)}, f32[3,9,48,256]{3,2,1,0:T(8,128)}, u32[]{:S(2)}) copy-start(f32[3,9,48,256]{3,2,1,0:T(8,128)} %copy-done.2) | copy-start | bytes 3981316
  26.9 11.9 %copy-start.6 = (f32[8,48,256]{2,1,0:T(8,128)S(1)}, f32[8,48,256]{2,1,0:T(8,128)}, u32[]{:S(2)}) copy-start(f32[8,48,256]{2,1,0:T(8,128)} %get-tuple-element.14) | copy-start | bytes 1179652
  27.2 8.1 %collective-permute-start.5 = (f32[3,10,1,258]{3,2,1,0:T(1,128)S(1)}, f32[3,10,1,258]{3,2,1,0:T(1,128)S(1)}, u32[]{:S(2)}, u32[]{:S(2)}) collective-permute-start(f32[3,10,1,258]{3,2,1,0:T(1,128)S(1)} %get-tuple-element.10), channel_id=1, source_target_pairs={{0,1},{1,2},{2,3},{4,5},{5,6},{6,7},{8,9},{9,10},{10,11},{12,13},{... | collective-permute-start | bytes 92888 | tf_op jit(solution)/shard_map/ppermute | solution.py:25
  33.4 5.4 %collective-permute-start.4 = (f32[3,10,1,258]{3,2,1,0:T(1,128)S(1)}, f32[3,10,1,258]{3,2,1,0:T(1,128)S(1)}, u32[]{:S(2)}, u32[]{:S(2)}) collective-permute-start(f32[3,10,1,258]{3,2,1,0:T(1,128)S(1)} %get-tuple-element.9), channel_id=1, source_target_pairs={{1,0},{2,1},{3,2},{5,4},{6,5},{7,6},{9,8},{10,9},{11,10},{13,12},{... | collective-permute-start | bytes 92888 | tf_op jit(solution)/shard_map/ppermute | solution.py:27
  44.4 1.2 %copy-start.11 = (s32[1,1,512]{2,1,0:T(1,128)S(1)}, s32[1,1,512]{2,1,0:T(1,128)}, u32[]{:S(2)}) copy-start(s32[1,1,512]{2,1,0:T(1,128)} %param.8) | copy-start | bytes 6148
  44.6 21.4 %copy-start.4 = (f32[4,1024]{0,1:T(8,128)S(1)}, f32[4,1024]{0,1:T(8,128)}, u32[]{:S(2)}) copy-start(f32[4,1024]{0,1:T(8,128)} %constant.24.clone.1) | copy-start | bytes 49156
  68.8 8.4 %all-to-all-start = ((f32[4,8,128]{2,0,1:T(4,128)}), f32[4,8,128]{2,0,1:T(4,128)S(1)}, u32[]{:S(2)}, u32[]{:S(2)}) async-start(f32[4,8,128]{2,0,1:T(4,128)} %copy.50), calls=%async_computation | async-start | bytes 32768 | tf_op jit(solution)/shard_map/all_to_all | solution.py:99
  88.1 5.3 %copy-start.7 = (f32[2,64,256]{2,1,0:T(8,128)S(1)}, f32[2,64,256]{2,1,0:T(8,128)}, u32[]{:S(2)}) copy-start(f32[2,64,256]{2,1,0:T(8,128)} %param.10) | copy-start | bytes 393220
  88.1 5.3 %copy-start.8 = (f32[64,256]{1,0:T(8,128)S(1)}, f32[64,256]{1,0:T(8,128)}, u32[]{:S(2)}) copy-start(f32[64,256]{1,0:T(8,128)} %param.9) | copy-start | bytes 196612
  88.1 5.3 %copy-start.9 = (s32[64,256]{1,0:T(8,128)S(1)}, s32[64,256]{1,0:T(8,128)}, u32[]{:S(2)}) copy-start(s32[64,256]{1,0:T(8,128)} %param.11) | copy-start | bytes 196612
  93.4 5.3 %collective-permute-start.6 = (f32[3,1,256]{2,1,0:T(1,128)S(1)}, f32[3,1,256]{2,1,0:T(1,128)S(1)}, u32[]{:S(2)}, u32[]{:S(2)}) collective-permute-start(f32[3,1,256]{2,1,0:T(1,128)S(1)} %get-tuple-element.30), channel_id=1, source_target_pairs={{8,0},{16,8},{24,16},{9,1},{17,9},{25,17},{10,2},{18,10},{26,18},{... | collective-permute-start | bytes 9224 | tf_op jit(solution)/shard_map/ppermute | solution.py:27
  94.7 4.7 %collective-permute-start.7 = (f32[3,1,256]{2,1,0:T(1,128)S(1)}, f32[3,1,256]{2,1,0:T(1,128)S(1)}, u32[]{:S(2)}, u32[]{:S(2)}) collective-permute-start(f32[3,1,256]{2,1,0:T(1,128)S(1)} %get-tuple-element.29), channel_id=1, source_target_pairs={{0,8},{8,16},{16,24},{1,9},{9,17},{17,25},{2,10},{10,18},{18,26},{... | collective-permute-start | bytes 9224 | tf_op jit(solution)/shard_map/ppermute | solution.py:25
  99.6 6.1 %collective-permute-start.8 = (f32[3,66,1]{2,1,0:T(8,128)S(1)}, f32[3,66,1]{2,1,0:T(8,128)S(1)}, u32[]{:S(2)}, u32[]{:S(2)}) collective-permute-start(f32[3,66,1]{2,1,0:T(8,128)S(1)} %get-tuple-element.28), channel_id=1, source_target_pairs={{1,0},{2,1},{3,2},{4,3},{5,4},{6,5},{7,6},{9,8},{10,9},{11,10},{12... | collective-permute-start | bytes 2384 | tf_op jit(solution)/shard_map/ppermute | solution.py:27
  103.5 3.7 %collective-permute-start.9 = (f32[3,66,1]{2,1,0:T(8,128)S(1)}, f32[3,66,1]{2,1,0:T(8,128)S(1)}, u32[]{:S(2)}, u32[]{:S(2)}) collective-permute-start(f32[3,66,1]{2,1,0:T(8,128)S(1)} %get-tuple-element.27), channel_id=1, source_target_pairs={{0,1},{1,2},{2,3},{3,4},{4,5},{5,6},{6,7},{8,9},{9,10},{10,11},{11... | collective-permute-start | bytes 2384 | tf_op jit(solution)/shard_map/ppermute | solution.py:25
Sparse Core Ops, SparseCore 0:
  45.7 19.0 reduce-scatter.3
where the time goes:
time: 118 us; the launch traced here: 115 us
  starting transfers between devices  34.3 us (29%)
  waiting for transfers between devices  30.8 us (26%)
  other arithmetic  19.4 us (16%)
  local copies, waits for them, and re-layouts  16.4 us (14%)
  between operations  14.5 us (12%)
    ppermute x5, starting transfers between devices, padded_2(): lax.ppermute(tail, axis, [(i, (i + 1) % count) for i in range(ends)])  20.2 us
    unnamed x2, waiting for transfers between devices  19.2 us
    scatter-add x1, other arithmetic, local(): source = jnp.zeros((3, far_x * far_y), jnp.float32).at[:, target].add(val...  10.6 us
    ppermute x5, starting transfers between devices, padded_2(): lax.ppermute(head, axis, [((i + 1) % count, i) for i in range(ends)])  9.67 us
    reshape x1, local copies, waits for them, and re-layouts, local(): source = jnp.zeros((3, far_x * far_y), jnp.float32).at[:, target].add(val...  5.26 us
    ppermute x5, waiting for transfers between devices, padded_2(): lax.ppermute(head, axis, [((i + 1) % count, i) for i in range(ends)])  4.85 us
    all_to_all x1, starting transfers between devices, local(): lax.all_to_all(buffer.reshape(4, owners, capacity), ('py', 'dz'), split_a...  4.38 us
    all_to_all x1, waiting for transfers between devices, local(): lax.all_to_all(buffer.reshape(4, owners, capacity), ('py', 'dz'), split_a...  4.04 us
  transfers between devices with their start and end apart: 12, of which 8 were waited for; matrix products, arithmetic and copies ran while one was open for 4% of the time, Pallas kernels for 0%

commit v1 on v0

v1 whole, which is shorter than its diff:
```python
import functools

import jax
import jax.numpy as jnp
from jax import lax
from jax.experimental import pallas as pl
from jax.experimental.pallas import tpu as pltpu
from jax.sharding import PartitionSpec as P

advect_coef = 0.25
diffuse_coef = 0.1
slope_coef = 0.5
flux_coef = 0.1
gravity = 1.0
column_height = 4.0

LANES = 128
PARTS = 3


def kernel(sizes, near, ids, far_in, wet_in, frac_out, far_out,
           x, nf, yedge, yhalo, zedge, zhalo, idall, sums, a_mat, b_mat, q, wet, fdep, fedge_r, fhalo_r, fedge_c, fhalo_c,
           fout, loc_sem, hs, hr, ids_s, ids_r, sum_s, sum_r):
    n_px, n_py, n_dz = sizes
    group = n_py * n_dz
    nx, nz, ny = near.shape[1:]
    fx, fy = wet_in.shape
    px, py, dz = lax.axis_index("px"), lax.axis_index("py"), lax.axis_index("dz")
    me = py * n_dz + dz

    def member(d):
        return {"px": px, "py": d // n_dz, "dz": d % n_dz}

    def peer(o):
        return lax.rem(me + o, group)

    def source(o):
        return lax.rem(me + group - o, group)

    up, down = {"px": px + 1, "py": py, "dz": dz}, {"px": px - 1, "py": py, "dz": dz}
    has_up, has_down = px < n_px - 1, px > 0

    barrier = pltpu.get_barrier_semaphore()
    for o in range(1, group):
        pl.semaphore_signal(barrier, inc=1, device_id=member(peer(o)))

    @pl.when(has_up)
    def _():
        pl.semaphore_signal(barrier, inc=1, device_id=up)

    @pl.when(has_down)
    def _():
        pl.semaphore_signal(barrier, inc=1, device_id=down)

    load_x = pltpu.make_async_copy(near, x.at[:, pl.ds(1, nx), pl.ds(8, nz), :], loc_sem.at[0])
    load_far = pltpu.make_async_copy(far_in, fdep, loc_sem.at[1])
    load_wet = pltpu.make_async_copy(wet_in, wet, loc_sem.at[2])
    load_ids = pltpu.make_async_copy(ids, idall.at[me], loc_sem.at[3])
    load_x.start()
    load_far.start()
    load_wet.start()
    load_ids.start()

    pl.semaphore_wait(barrier, group - 1 + has_up.astype(jnp.int32) + has_down.astype(jnp.int32))

    def send(src, dst, i, where):
        return pltpu.make_async_remote_copy(src_ref=src, dst_ref=dst, send_sem=hs.at[i], recv_sem=hr.at[i], device_id=where)

    rows = pl.ds(8, nz)
    x_up = send(near.at[:, nx - 1], x.at[:, 0, rows, :], 0, up)
    x_down = send(near.at[:, 0], x.at[:, nx + 1, rows, :], 1, down)
    y_up = send(yedge.at[0], yhalo.at[0], 2, {"px": px, "py": py + 1, "dz": dz})
    y_down = send(yedge.at[1], yhalo.at[1], 3, {"px": px, "py": py - 1, "dz": dz})
    z_up = send(zedge.at[0], zhalo.at[0], 4, {"px": px, "py": py, "dz": dz + 1})
    z_down = send(zedge.at[1], zhalo.at[1], 5, {"px": px, "py": py, "dz": dz - 1})
    fr_up = send(fedge_r.at[0], fhalo_r.at[0], 6, up)
    fr_down = send(fedge_r.at[1], fhalo_r.at[1], 7, down)
    fc_up = send(fedge_c.at[0], fhalo_c.at[0], 8, member(me + 1))
    fc_down = send(fedge_c.at[1], fhalo_c.at[1], 9, member(me - 1))
    near_y = ((y_up, py < n_py - 1, py > 0, yhalo.at[0]), (y_down, py > 0, py < n_py - 1, yhalo.at[1]))
    near_z = ((z_up, dz < n_dz - 1, dz > 0, zhalo.at[0]), (z_down, dz > 0, dz < n_dz - 1, zhalo.at[1]))
    near_x = ((x_up, has_up, has_down, x.at[:, 0]), (x_down, has_down, has_up, x.at[:, nx + 1]))
    far_r = ((fr_up, has_up, has_down, fhalo_r.at[0]), (fr_down, has_down, has_up, fhalo_r.at[1]))
    far_c = ((fc_up, me < group - 1, me > 0, fhalo_c.at[0]), (fc_down, me > 0, me < group - 1, fhalo_c.at[1]))

    def start(pairs):
        for copy, out, _, _ in pairs:
            pl.when(out)(copy.start)

    def clear(pairs):
        for _, _, into, halo in pairs:
            @pl.when(jnp.logical_not(into))
            def _():
                halo[...] = jnp.zeros(halo.shape, jnp.float32)

    def arrive(pairs):
        for copy, _, into, _ in pairs:
            pl.when(into)(copy.wait_recv)

    def sent(pairs):
        for copy, out, _, _ in pairs:
            pl.when(out)(copy.wait_send)

    start(near_x)
    for pairs in (near_x, near_y, near_z, far_r, far_c):
        clear(pairs)

    load_x.wait()
    lane = lax.broadcasted_iota(jnp.int32, (nz, LANES), 1)
    for f in range(3):
        for i in range(nx):
            zedge[0, f, pl.ds(i, 1), :] = x[f, i + 1, pl.ds(nz + 7, 1), :]
            zedge[1, f, pl.ds(i, 1), :] = x[f, i + 1, pl.ds(8, 1), :]
    start(near_z)
    high = jnp.zeros((nz, LANES), jnp.float32)
    low = jnp.zeros((nz, LANES), jnp.float32)
    for i in range(nx):
        for f in range(3):
            k = 3 * i + f
            high = jnp.where(lane == k, pltpu.roll(x[f, i + 1, rows, ny - LANES:], (k + 1) % LANES, 1), high)
            first = x[f, i + 1, rows, :LANES]
            low = jnp.where(lane == k, pltpu.roll(first, k, 1) if k else first, low)
    yedge[0] = high
    yedge[1] = low
    start(near_y)

    load_ids.wait()

    def id_copy(o, d):
        return pltpu.make_async_remote_copy(
            src_ref=idall.at[me], dst_ref=idall.at[d], send_sem=ids_s.at[o], recv_sem=ids_r.at[o], device_id=member(peer(o)))

    for o in range(1, group):
        id_copy(o, me).start()

    arrive(near_z)
    for f in range(3):
        for i in range(nx):
            x[f, i + 1, pl.ds(7, 1), :] = zhalo[0, f, pl.ds(i, 1), :]
            x[f, i + 1, pl.ds(nz + 8, 1), :] = zhalo[1, f, pl.ds(i, 1), :]
    arrive(near_y)

    col = lax.broadcasted_iota(jnp.int32, (8, ny), 1)

    def plane(i):
        total = [jnp.zeros((8, ny), jnp.float32) for _ in range(3)]
        shift = (LANES - 3 * i) % LANES if isinstance(i, int) else lax.rem(LANES - 3 * i, LANES)
        for c in range(0, nz, 8):
            here = pl.ds(8 + c, 8)
            ylo = pltpu.roll(yhalo[0, pl.ds(c, 8), :], shift, 1)
            yhi = pltpu.roll(yhalo[1, pl.ds(c, 8), :], shift, 1)
            u, v = x[1, i + 1, here, :], x[2, i + 1, here, :]
            moved, slopes = [], None
            for f in range(3):
                mid = x[f, i + 1, here, :]
                xp, xm = x[f, i + 2, here, :], x[f, i, here, :]
                zp, zm = x[f, i + 1, pl.ds(9 + c, 8), :], x[f, i + 1, pl.ds(7 + c, 8), :]
                yp = jnp.where(col == ny - 1, yhi[:, f:f + 1], pltpu.roll(mid, ny - 1, 1))
                ym = jnp.where(col == 0, ylo[:, f:f + 1], pltpu.roll(mid, 1, 1))
                dx, dy = xp - xm, yp - ym
                lap = xp + xm + yp + ym + zp + zm - 6.0 * mid
                moved.append(mid - advect_coef * (u * dx + v * dy) + diffuse_coef * lap)
                if f == 0:
                    slopes = (dx, dy)
            nf[i, pl.ds(c, 8), :] = moved[0]
            total[0] += moved[0]
            total[1] += moved[0] * (moved[1] - slope_coef * slopes[0])
            total[2] += moved[0] * (moved[2] - slope_coef * slopes[1])
        for f in range(3):
            sums[me, f, pl.ds(i, 1), :] = jnp.sum(total[f], axis=0, keepdims=True)

    def inner(i, carry):
        plane(i)
        return carry

    lax.fori_loop(1, nx - 1, inner, 0)

    for o in range(1, group):
        id_copy(o, source(o)).wait_recv()
    row_at = []
    line = lax.broadcasted_iota(jnp.int32, (fy, ny), 0)
    for p in range(n_py):
        owner, land = idall[p * n_dz, 0], idall[p * n_dz, 1]
        for e in range(1, n_dz):
            owner = owner + idall[p * n_dz + e, 0]
            land = land + idall[p * n_dz + e, 1]
        row = lax.div(land, jnp.full_like(land, fy)) if fy & (fy - 1) else lax.shift_right_logical(land, jnp.full_like(land, fy.bit_length() - 1))
        at = land - row * fy
        row_at.append(jnp.where(owner == me, row, -1))
        for i in range(nx):
            b = (p * nx + i) * ny
            b_mat[:, pl.ds(b, ny)] = jnp.where(line == at[i:i + 1, :], 1.0, 0.0).astype(jnp.bfloat16)

    arrive(near_x)
    plane(0)
    plane(nx - 1)

    def sum_copy(o, d):
        return pltpu.make_async_remote_copy(
            src_ref=sums.at[me], dst_ref=sums.at[d], send_sem=sum_s.at[o], recv_sem=sum_r.at[o], device_id=member(peer(o)))

    for o in range(1, group):
        sum_copy(o, me).start()
    save_frac = pltpu.make_async_copy(nf, frac_out, loc_sem.at[4])
    save_frac.start()
    load_far.wait()
    load_wet.wait()
    for o in range(1, group):
        sum_copy(o, source(o)).wait_recv()

    per_column = column_height / (nz * n_dz)
    cell_row = lax.broadcasted_iota(jnp.int32, (fx, ny), 0)
    for p in range(n_py):
        parts = []
        for f in range(3):
            rest = sums[p * n_dz, f]
            for e in range(1, n_dz):
                rest = rest + sums[p * n_dz + e, f]
            rest = rest * per_column
            for s in range(PARTS):
                part = rest.astype(jnp.bfloat16).astype(jnp.float32)
                rest = rest - part
                parts.append(part)
        for i in range(nx):
            b = (p * nx + i) * ny
            hit = cell_row == row_at[p][i:i + 1, :]
            for k, part in enumerate(parts):
                a_mat[pl.ds(k * fx, fx), pl.ds(b, ny)] = jnp.where(hit, part[i:i + 1, :], 0.0).astype(jnp.bfloat16)
    landed = lax.dot_general(a_mat[...], b_mat[...], (((1,), (1,)), ((), ())), preferred_element_type=jnp.float32)
    dry = wet[...].astype(jnp.float32)
    for f in range(3):
        state = fdep[f]
        for s in range(PARTS):
            k = f * PARTS + s
            state = state + landed[k * fx:(k + 1) * fx, :]
        if f:
            state = state * dry
        q[f, pl.ds(8, fx), :] = state
        fedge_r[0, pl.ds(f, 1), :] = state[fx - 1:fx, :]
        fedge_r[1, pl.ds(f, 1), :] = state[0:1, :]
    start(far_r)
    lane = lax.broadcasted_iota(jnp.int32, (fx, LANES), 1)
    high = jnp.zeros((fx, LANES), jnp.float32)
    low = jnp.zeros((fx, LANES), jnp.float32)
    for f in range(3):
        high = jnp.where(lane == f, pltpu.roll(q[f, pl.ds(8, fx), fy - LANES:], f + 1, 1), high)
        first = q[f, pl.ds(8, fx), :LANES]
        low = jnp.where(lane == f, pltpu.roll(first, f, 1) if f else first, low)
    fedge_c[0] = high
    fedge_c[1] = low
    start(far_c)

    def fluxes(h, hu, hv, divisor):
        inverse = 1.0 / divisor
        press = 0.5 * gravity * h * h
        return hu * hu * inverse + press, hu * hv * inverse, hv * hv * inverse + press

    for c in range(8, fx + 8, 8):
        here = pl.ds(c, 8)
        h, hu, hv = q[0, here, :], q[1, here, :], q[2, here, :]
        for k, flux in enumerate(fluxes(h, hu, hv, h)):
            q[3 + k, here, :] = flux

    arrive(far_r)
    for side, there, at in ((0, has_down, 7), (1, has_up, fx + 8)):
        h, hu, hv = (fhalo_r[side, pl.ds(f, 1), :] for f in range(3))
        for k, value in enumerate((h, hu, hv) + fluxes(h, hu, hv, jnp.where(there, h, 1.0))):
            q[k, pl.ds(at, 1), :] = value
    arrive(far_c)
    col = lax.broadcasted_iota(jnp.int32, (8, fy), 1)
    for c in range(0, fx, 8):
        here = pl.ds(8 + c, 8)
        outer = []
        for side, there in ((0, me > 0), (1, me < group - 1)):
            block = fhalo_c[side, pl.ds(c, 8), :]
            h, hu, hv = block, pltpu.roll(block, LANES - 1, 1), pltpu.roll(block, LANES - 2, 1)
            outer.append([z[:, 0:1] for z in (h, hu, hv) + fluxes(h, hu, hv, jnp.where(there, h, 1.0))])

        def beside(k):
            mid = q[k, here, :]
            return (jnp.where(col == fy - 1, outer[1][k], pltpu.roll(mid, fy - 1, 1)),
                    jnp.where(col == 0, outer[0][k], pltpu.roll(mid, 1, 1)))

        above = [q[k, pl.ds(9 + c, 8), :] for k in range(5)]
        below = [q[k, pl.ds(7 + c, 8), :] for k in range(5)]
        pairs = [beside(0), beside(1), beside(2), None, beside(4), beside(5)]
        for f, (xk, yk) in enumerate(((1, 2), (3, 4), (4, 5))):
            mean = 0.25 * (above[f] + below[f] + pairs[f][0] + pairs[f][1])
            fout[f, pl.ds(c, 8), :] = (
                mean - flux_coef * (above[xk] - below[xk]) - flux_coef * (pairs[yk][0] - pairs[yk][1]))
    save_far = pltpu.make_async_copy(fout, far_out, loc_sem.at[5])
    save_far.start()

    for pairs in (near_x, near_y, near_z, far_r, far_c):
        sent(pairs)
    for o in range(1, group):
        id_copy(o, me).wait_send()
        sum_copy(o, me).wait_send()
    save_frac.wait()
    save_far.wait()


def solution(mesh):
    sizes = tuple(mesh.shape[axis] for axis in ("px", "py", "dz"))
    n_px, n_py, n_dz = sizes
    group = n_py * n_dz

    def local(near_state, column_owner, landing, far_depth, far_flows, wet_mask):
        _, nx, nz, ny = near_state.shape
        fx, fy = far_depth.shape
        qy = ny // n_dz
        ids = jnp.stack([column_owner.reshape(nx, qy), landing.reshape(nx, qy)])
        ids = lax.dynamic_update_slice(
            jnp.zeros((2, nx, ny), jnp.int32), ids, (0, 0, lax.axis_index("dz") * qy))
        far = jnp.concatenate([far_depth[None], far_flows])
        anywhere = pl.BlockSpec(memory_space=pl.ANY)
        f32 = jnp.float32
        columns = n_py * nx * ny
        return pl.pallas_call(
            functools.partial(kernel, sizes),
            out_shape=(jax.ShapeDtypeStruct((nx, nz, ny), f32), jax.ShapeDtypeStruct((3, fx, fy), f32)),
            in_specs=[anywhere] * 4,
            out_specs=(anywhere, anywhere),
            scratch_shapes=[
                pltpu.VMEM((3, nx + 2, nz + 16, ny), f32),
                pltpu.VMEM((nx, nz, ny), f32),
                pltpu.VMEM((2, nz, LANES), f32),
                pltpu.VMEM((2, nz, LANES), f32),
                pltpu.VMEM((2, 3, nx, ny), f32),
                pltpu.VMEM((2, 3, nx, ny), f32),
                pltpu.VMEM((group, 2, nx, ny), jnp.int32),
                pltpu.VMEM((group, 3, nx, ny), f32),
                pltpu.VMEM((3 * PARTS * fx, columns), jnp.bfloat16),
                pltpu.VMEM((fy, columns), jnp.bfloat16),
                pltpu.VMEM((6, fx + 16, fy), f32),
                pltpu.VMEM((fx, fy), jnp.int32),
                pltpu.VMEM((3, fx, fy), f32),
                pltpu.VMEM((2, 8, fy), f32),
                pltpu.VMEM((2, 8, fy), f32),
                pltpu.VMEM((2, fx, LANES), f32),
                pltpu.VMEM((2, fx, LANES), f32),
                pltpu.VMEM((3, fx, fy), f32),
                pltpu.SemaphoreType.DMA((6,)),
                pltpu.SemaphoreType.DMA((10,)),
                pltpu.SemaphoreType.DMA((10,)),
                pltpu.SemaphoreType.DMA((group,)),
                pltpu.SemaphoreType.DMA((group,)),
                pltpu.SemaphoreType.DMA((group,)),
                pltpu.SemaphoreType.DMA((group,)),
            ],
            compiler_params=pltpu.CompilerParams(
                collective_id=0, has_side_effects=True, vmem_limit_bytes=48 * 1024 * 1024),
        )(near_state, ids, far, wet_mask)

    return jax.shard_map(
        local,
        mesh=mesh,
        in_specs=(
            P(None, "px", "dz", "py"),
            P("px", ("py", "dz"), None, None),
            P("px", ("py", "dz"), None),
            P("px", ("py", "dz")),
            P(None, "px", ("py", "dz")),
            P("px", ("py", "dz")),
        ),
        out_specs=(P("px", "dz", "py"), P(None, "px", ("py", "dz"))),
        check_vma=False,
    )
```

time: 118 us -> 28.4 us (0.24); the launches traced: 115 us -> 28.1 us
  starting transfers between devices: 34.3 us -> 0 us
  waiting for transfers between devices: 30.8 us -> 0 us
  Pallas kernels: 0 us -> 19.2 us
  other arithmetic: 19.4 us -> 3.62 us
  between operations: 14.5 us -> 0.66 us
  local copies, waits for them, and re-layouts: 16.4 us -> 4.61 us
    ppermute x10 -> x0, starting transfers between devices: 29.9 us -> none  [the longest x5 20.2 us: padded_2(): lax.ppermute(tail, axis, [(i, (i + 1) % count) for i in range(ends)])]
    pallas_call x0 -> x1, Pallas kernels: none -> 19.2 us  [local(): pl.pallas_call(functools.partial(kernel, sizes), out_shape=(jax.ShapeDtyp...]
    unnamed x2 -> x0, waiting for transfers between devices: 19.2 us -> none
    scatter-add x1 -> x0, other arithmetic: 10.6 us -> none  [local(): source = jnp.zeros((3, far_x * far_y), jnp.float32).at[:, target].add(val...]
    ppermute x10 -> x0, waiting for transfers between devices: 7.52 us -> none  [the longest x5 4.85 us: padded_2(): lax.ppermute(head, axis, [((i + 1) % count, i) for i in range(ends)])]
    reshape x3 -> x0, local copies, waits for them, and re-layouts: 6.14 us -> none  [the longest x1 5.26 us: local(): source = jnp.zeros((3, far_x * far_y), jnp.float32).at[:, target].add(val...]
    all_to_all x1 -> x0, starting transfers between devices: 4.38 us -> none  [local(): lax.all_to_all(buffer.reshape(4, owners, capacity), ('py', 'dz'), split_a...]
    all_to_all x1 -> x0, waiting for transfers between devices: 4.04 us -> none  [local(): lax.all_to_all(buffer.reshape(4, owners, capacity), ('py', 'dz'), split_a...]
  transfers between devices with their start and end apart: 12 -> 0, of which waited for: 8 -> 0; matrix products, arithmetic and copies ran while one was open for 4% -> 0% of each run, Pallas kernels for 0% -> 0%
where the time goes in v1:
time: 28.4 us; the launch traced here: 28.1 us
  Pallas kernels  19.2 us (68%)
  local copies, waits for them, and re-layouts  4.61 us (16%)
  other arithmetic  3.62 us (13%)
  between operations  0.66 us (2%)
    pallas_call x1, Pallas kernels, local(): pl.pallas_call(functools.partial(kernel, sizes), out_shape=(jax.ShapeDtyp...  19.2 us
    unnamed x7, local copies, waits for them, and re-layouts  4.04 us
    unnamed x2, other arithmetic  2.69 us
    concatenate x1, other arithmetic, local(): far = jnp.concatenate([far_depth[None], far_flows])  0.93 us

profile of v1, /device:TPU:1, one launch (start us, length us, event | category | flops | bytes accessed | tf_op | source)
XLA Modules:
  0.0 28.1 jit_solution(14603040847657483779)
XLA Ops:
  0.6 0.5 %broadcast.6 = s32[]{:T(128)} broadcast(s32[]{:T(128)} %constant.4.clone.1), dimensions={} | broadcast | bytes 8 | tf_op args[2]
  1.1 1.3 %reduce.7 = s32[512]{0:T(512)S(1)} reduce(s32[1,1,512,1]{2,3,1,0:T(1,128)} %param.7, s32[]{:T(128)} %broadcast.6), dimensions={0,1,3}, to_apply=%param.7.reduce_sub_computation.3 | reduce | bytes 4100 | tf_op args[1]
  2.5 1.3 %reduce.6 = s32[512]{0:T(512)S(1)} reduce(s32[1,1,512]{2,1,0:T(1,128)} %param.8, s32[]{:T(128)} %broadcast.6), dimensions={0,1}, to_apply=%param.8.reduce_sub_computation.3 | reduce | bytes 4100 | tf_op args[2]
  3.8 0.1 stack_reshape.7
  3.9 0.1 stack_reshape.6
  4.0 0.4 %dynamic_update_slice.3.ids = s32[2,8,256]{2,1,0:T(8,128)S(1)} dynamic-update-slice(s32[2,8,256]{2,1,0:T(8,128)S(1)} %broadcast_in_dim.6, s32[2,8,64]{2,1,0:T(8,128)S(1)} %pad_add_fusion, s32[]{:T(128)} %constant.4.clone.1, s32[]{:T(128)} %constant.4.clone.1, s32[]{:T(128)S(6)} %select_n.3) | dynamic-update-slice | bytes 8196 | tf_op jit(solution)/shard_map/dynamic_update_slice | solution.py:313
  4.4 0.9 %pad_maximum_fusion.far_in = f32[3,64,256]{2,1,0:T(8,128)S(1)} fusion(f32[2,64,256]{2,1,0:T(8,128)} %param.10, f32[1,64,256]{2,1,0:T(8,128)} %bitcast.2), kind=kLoop, calls=%fused_computation | loop fusion | flops 49152 | bytes 393216 | tf_op jit(solution)/shard_map/concatenate | solution.py:315
  5.3 0.0 copy-start
  5.4 1.3 %copy-done = f32[3,8,48,256]{3,2,1,0:T(8,128)S(1)} copy-done((f32[3,8,48,256]{3,2,1,0:T(8,128)S(1)}, f32[3,8,48,256]{3,2,1,0:T(8,128)}, u32[]{:S(2)}) %copy-start) | copy-done | bytes 1179672
  6.6 0.0 copy-start.1
  6.6 0.8 %copy-done.1 = s32[64,256]{1,0:T(8,128)S(1)} copy-done((s32[64,256]{1,0:T(8,128)S(1)}, s32[64,256]{1,0:T(8,128)}, u32[]{:S(2)}) %copy-start.1) | copy-done | bytes 65560
  7.5 19.2 %shard_map.77 = (f32[8,48,256]{2,1,0:T(8,128)S(1)}, f32[3,64,256]{2,1,0:T(8,128)S(1)}) custom-call(f32[3,8,48,256]{3,2,1,0:T(8,128)S(1)} %copy-done, s32[2,8,256]{2,1,0:T(8,128)S(1)} %dynamic_update_slice.3.ids, f32[3,64,256]{2,1,0:T(8,128)S(1)} %pad_maximum_fusion.far_in, s32[64,256]{1,0:T(8,128)S(1)} %copy-done.1), custom_call_target="tpu_custom_call" | custom-call | tf_op jit(solution)/shard_map/pallas_call | solution.py:319
  26.7 0.7 %copy.11 = f32[8,48,256]{2,1,0:T(8,128)} copy(f32[8,48,256]{2,1,0:T(8,128)S(1)} %get-tuple-element.4) | data formatting | bytes 786432
  27.5 0.7 %copy.12 = f32[3,64,256]{2,1,0:T(8,128)} copy(f32[3,64,256]{2,1,0:T(8,128)S(1)} %get-tuple-element.5) | data formatting | bytes 393216
  (2 shorter events, 0.0 us)
Async XLA Ops:
  5.3 1.3 %copy-start = (f32[3,8,48,256]{3,2,1,0:T(8,128)S(1)}, f32[3,8,48,256]{3,2,1,0:T(8,128)}, u32[]{:S(2)}) copy-start(f32[3,8,48,256]{3,2,1,0:T(8,128)} %near.1) | copy-start | bytes 3538948
  6.6 0.8 %copy-start.1 = (s32[64,256]{1,0:T(8,128)S(1)}, s32[64,256]{1,0:T(8,128)}, u32[]{:S(2)}) copy-start(s32[64,256]{1,0:T(8,128)} %wet_in.1) | copy-start | bytes 196612

commit v2 on v1

--- a/solution.py
+++ b/solution.py
@@ -15,12 +15,12 @@
 column_height = 4.0
 
 LANES = 128
-PARTS = 3
-
-
-def kernel(sizes, near, ids, far_in, wet_in, frac_out, far_out,
-           x, nf, yedge, yhalo, zedge, zhalo, idall, sums, a_mat, b_mat, q, wet, fdep, fedge_r, fhalo_r, fedge_c, fhalo_c,
-           fout, loc_sem, hs, hr, ids_s, ids_r, sum_s, sum_r):
+PARTS = 2
+
+
+def kernel(sizes, near, own_in, land_in, dep_in, flow_in, wet_in, frac_out, far_out,
+           x, nf, fout, idraw, yedge, yhalo, zedge, zhalo, idall, sums, a_mat, b_mat, q, wet, fdep, fedge_r, fhalo_r, fedge_c, fhalo_c,
+           loc_sem, hs, hr, ids_s, ids_r, sum_s, sum_r):
     n_px, n_py, n_dz = sizes
     group = n_py * n_dz
     nx, nz, ny = near.shape[1:]
@@ -53,13 +53,14 @@
         pl.semaphore_signal(barrier, inc=1, device_id=down)
 
     load_x = pltpu.make_async_copy(near, x.at[:, pl.ds(1, nx), pl.ds(8, nz), :], loc_sem.at[0])
-    load_far = pltpu.make_async_copy(far_in, fdep, loc_sem.at[1])
+    load_dep = pltpu.make_async_copy(dep_in, fdep.at[0], loc_sem.at[1])
+    load_flow = pltpu.make_async_copy(flow_in, fdep.at[pl.ds(1, 2)], loc_sem.at[4])
     load_wet = pltpu.make_async_copy(wet_in, wet, loc_sem.at[2])
-    load_ids = pltpu.make_async_copy(ids, idall.at[me], loc_sem.at[3])
-    load_x.start()
-    load_far.start()
-    load_wet.start()
-    load_ids.start()
+    load_own = pltpu.make_async_copy(own_in.at[0], idraw.at[0], loc_sem.at[3])
+    load_land = pltpu.make_async_copy(land_in.at[0], idraw.at[1], loc_sem.at[5])
+    loads = (load_x, load_own, load_land, load_dep, load_flow, load_wet)
+    for load in loads:
+        load.start()
 
     pl.semaphore_wait(barrier, group - 1 + has_up.astype(jnp.int32) + has_down.astype(jnp.int32))
 
@@ -124,7 +125,20 @@
     yedge[1] = low
     start(near_y)
 
-    load_ids.wait()
+    load_own.wait()
+    load_land.wait()
+    count = idraw.shape[2]
+    qy = count // nx
+    level = lax.broadcasted_iota(jnp.int32, (nx, ny), 0)
+    along = lax.broadcasted_iota(jnp.int32, (nx, ny), 1)
+    mine = jnp.logical_and(along >= dz * qy, along < (dz + 1) * qy)
+    for t in range(2):
+        raw = jnp.broadcast_to(idraw[t], (nx, count))
+        placed = jnp.zeros((nx, ny), jnp.int32)
+        for i in range(nx):
+            turned = pltpu.roll(raw, lax.rem(dz * qy + (count - i * qy), count), 1)[:, :ny]
+            placed = jnp.where(jnp.logical_and(level == i, mine), turned, placed)
+        idall[me, t] = placed
 
     def id_copy(o, d):
         return pltpu.make_async_remote_copy(
@@ -201,9 +215,10 @@
 
     for o in range(1, group):
         sum_copy(o, me).start()
-    save_frac = pltpu.make_async_copy(nf, frac_out, loc_sem.at[4])
+    save_frac = pltpu.make_async_copy(nf, frac_out, loc_sem.at[6])
     save_frac.start()
-    load_far.wait()
+    load_dep.wait()
+    load_flow.wait()
     load_wet.wait()
     for o in range(1, group):
         sum_copy(o, source(o)).wait_recv()
@@ -288,9 +303,9 @@
             mean = 0.25 * (above[f] + below[f] + pairs[f][0] + pairs[f][1])
             fout[f, pl.ds(c, 8), :] = (
                 mean - flux_coef * (above[xk] - below[xk]) - flux_coef * (pairs[yk][0] - pairs[yk][1]))
-    save_far = pltpu.make_async_copy(fout, far_out, loc_sem.at[5])
+
+    save_far = pltpu.make_async_copy(fout, far_out, loc_sem.at[7])
     save_far.start()
-
     for pairs in (near_x, near_y, near_z, far_r, far_c):
         sent(pairs)
     for o in range(1, group):
@@ -306,24 +321,21 @@
     group = n_py * n_dz
 
     def local(near_state, column_owner, landing, far_depth, far_flows, wet_mask):
-        _, nx, nz, ny = near_state.shape
+        nx, nz, ny = near_state.shape[1:]
         fx, fy = far_depth.shape
-        qy = ny // n_dz
-        ids = jnp.stack([column_owner.reshape(nx, qy), landing.reshape(nx, qy)])
-        ids = lax.dynamic_update_slice(
-            jnp.zeros((2, nx, ny), jnp.int32), ids, (0, 0, lax.axis_index("dz") * qy))
-        far = jnp.concatenate([far_depth[None], far_flows])
-        anywhere = pl.BlockSpec(memory_space=pl.ANY)
+        kept = pl.BlockSpec(memory_space=pltpu.HBM)
         f32 = jnp.float32
         columns = n_py * nx * ny
         return pl.pallas_call(
             functools.partial(kernel, sizes),
             out_shape=(jax.ShapeDtypeStruct((nx, nz, ny), f32), jax.ShapeDtypeStruct((3, fx, fy), f32)),
-            in_specs=[anywhere] * 4,
-            out_specs=(anywhere, anywhere),
+            in_specs=[kept] * 6,
+            out_specs=(kept, kept),
             scratch_shapes=[
                 pltpu.VMEM((3, nx + 2, nz + 16, ny), f32),
                 pltpu.VMEM((nx, nz, ny), f32),
+                pltpu.VMEM((3, fx, fy), f32),
+                pltpu.VMEM((2, 1, landing.shape[2]), jnp.int32),
                 pltpu.VMEM((2, nz, LANES), f32),
                 pltpu.VMEM((2, nz, LANES), f32),
                 pltpu.VMEM((2, 3, nx, ny), f32),
@@ -339,8 +351,7 @@
                 pltpu.VMEM((2, 8, fy), f32),
                 pltpu.VMEM((2, fx, LANES), f32),
                 pltpu.VMEM((2, fx, LANES), f32),
-                pltpu.VMEM((3, fx, fy), f32),
-                pltpu.SemaphoreType.DMA((6,)),
+                pltpu.SemaphoreType.DMA((8,)),
                 pltpu.SemaphoreType.DMA((10,)),
                 pltpu.SemaphoreType.DMA((10,)),
                 pltpu.SemaphoreType.DMA((group,)),
@@ -349,8 +360,8 @@
                 pltpu.SemaphoreType.DMA((group,)),
             ],
             compiler_params=pltpu.CompilerParams(
-                collective_id=0, has_side_effects=True, vmem_limit_bytes=48 * 1024 * 1024),
-        )(near_state, ids, far, wet_mask)
+                collective_id=0, has_side_effects=True, vmem_limit_bytes=63 * 1024 * 1024),
+        )(near_state, column_owner.reshape(landing.shape), landing, far_depth, far_flows, wet_mask)
 
     return jax.shard_map(
         local,

time: 28.4 us -> 23.7 us (0.83)
  other arithmetic: 3.62 us -> 0 us
  local copies, waits for them, and re-layouts: 4.61 us -> 3.38 us
  Pallas kernels: 19.2 us -> 19.5 us
    unnamed x2 -> x0, other arithmetic: 2.69 us -> none
    concatenate x1 -> x0, other arithmetic: 0.93 us -> none  [local(): far = jnp.concatenate([far_depth[None], far_flows])]
    unnamed x7 -> x2, local copies, waits for them, and re-layouts: 4.04 us -> 3.38 us
    dynamic_update_slice x1 -> x0, local copies, waits for them, and re-layouts: 0.41 us -> none  [local(): lax.dynamic_update_slice(jnp.zeros((2, nx, ny), jnp.int32), ids, (0, 0, l...]
    pallas_call x1, Pallas kernels: 19.2 us -> 19.5 us  [local(): pl.pallas_call(functools.partial(kernel, sizes), out_shape=(jax.ShapeDtyp...]
where the time goes in v2:
time: 23.7 us; the launch traced here: 23.6 us
  Pallas kernels  19.5 us (82%)
  local copies, waits for them, and re-layouts  3.38 us (14%)
  between operations  0.64 us (3%)
    pallas_call x1, Pallas kernels, local(): pl.pallas_call(functools.partial(kernel, sizes), out_shape=(jax.ShapeDtyp...  19.5 us
    unnamed x2, local copies, waits for them, and re-layouts  3.38 us

profile of v2, /device:TPU:1, one launch (start us, length us, event | category | flops | bytes accessed | tf_op | source)
XLA Modules:
  0.0 23.6 jit_solution(2253268381044935620)
XLA Ops:
  0.6 19.5 %shard_map.77 = (f32[8,48,256]{2,1,0:T(8,128)}, f32[3,64,256]{2,1,0:T(8,128)}) custom-call(f32[3,8,48,256]{3,2,1,0:T(8,128)} %near.1, s32[1,1,512]{2,1,0:T(1,128)} %bitcast.1, s32[1,1,512]{2,1,0:T(1,128)} %land_in.1, f32[64,256]{1,0:T(8,128)} %dep_in.1, f32[2,64,256]{2,1,0:T(8,128)} %flow_in.1, s32[64,256]{1,0:T(8,128)} %wet_in.1), custom_call_target="tpu_custom_call" | custom-call | tf_op jit(solution)/shard_map/pallas_call | solution.py:329
  20.2 1.8 %copy.10 = f32[8,48,256]{2,1,0:T(8,128)} copy(f32[8,48,256]{2,1,0:T(8,128)} %get-tuple-element.4) | data formatting | bytes 786432
  21.9 1.6 %copy.11 = f32[3,64,256]{2,1,0:T(8,128)} copy(f32[3,64,256]{2,1,0:T(8,128)} %get-tuple-element.5) | data formatting | bytes 393216

commit v3 on v2

--- a/solution.py
+++ b/solution.py
@@ -18,8 +18,8 @@
 PARTS = 2
 
 
-def kernel(sizes, near, own_in, land_in, dep_in, flow_in, wet_in, frac_out, far_out,
-           x, nf, fout, idraw, yedge, yhalo, zedge, zhalo, idall, sums, a_mat, b_mat, q, wet, fdep, fedge_r, fhalo_r, fedge_c, fhalo_c,
+def kernel(sizes, near, own_in, land_in, dep_in, flow_in, wet_in, nf, fout,
+           x, idraw, yedge, yhalo, zedge, zhalo, idall, sums, a_mat, b_mat, q, wet, fdep, fedge_r, fhalo_r, fedge_c, fhalo_c,
            loc_sem, hs, hr, ids_s, ids_r, sum_s, sum_r):
     n_px, n_py, n_dz = sizes
     group = n_py * n_dz
@@ -215,8 +215,6 @@
 
     for o in range(1, group):
         sum_copy(o, me).start()
-    save_frac = pltpu.make_async_copy(nf, frac_out, loc_sem.at[6])
-    save_frac.start()
     load_dep.wait()
     load_flow.wait()
     load_wet.wait()
@@ -304,15 +302,11 @@
             fout[f, pl.ds(c, 8), :] = (
                 mean - flux_coef * (above[xk] - below[xk]) - flux_coef * (pairs[yk][0] - pairs[yk][1]))
 
-    save_far = pltpu.make_async_copy(fout, far_out, loc_sem.at[7])
-    save_far.start()
     for pairs in (near_x, near_y, near_z, far_r, far_c):
         sent(pairs)
     for o in range(1, group):
         id_copy(o, me).wait_send()
         sum_copy(o, me).wait_send()
-    save_frac.wait()
-    save_far.wait()
 
 
 def solution(mesh):
@@ -328,13 +322,11 @@
         columns = n_py * nx * ny
         return pl.pallas_call(
             functools.partial(kernel, sizes),
-            out_shape=(jax.ShapeDtypeStruct((nx, nz, ny), f32), jax.ShapeDtypeStruct((3, fx, fy), f32)),
+            out_shape=(pltpu.VMEM((nx, nz, ny), f32), pltpu.VMEM((3, fx, fy), f32)),
             in_specs=[kept] * 6,
-            out_specs=(kept, kept),
+            out_specs=(pl.BlockSpec(memory_space=pltpu.VMEM),) * 2,
             scratch_shapes=[
                 pltpu.VMEM((3, nx + 2, nz + 16, ny), f32),
-                pltpu.VMEM((nx, nz, ny), f32),
-                pltpu.VMEM((3, fx, fy), f32),
                 pltpu.VMEM((2, 1, landing.shape[2]), jnp.int32),
                 pltpu.VMEM((2, nz, LANES), f32),
                 pltpu.VMEM((2, nz, LANES), f32),
@@ -360,7 +352,7 @@
                 pltpu.SemaphoreType.DMA((group,)),
             ],
             compiler_params=pltpu.CompilerParams(
-                collective_id=0, has_side_effects=True, vmem_limit_bytes=63 * 1024 * 1024),
+                collective_id=0, has_side_effects=True, vmem_limit_bytes=62 * 1024 * 1024),
         )(near_state, column_owner.reshape(landing.shape), landing, far_depth, far_flows, wet_mask)
 
     return jax.shard_map(

time: 23.7 us -> 21.1 us (0.89)
  local copies, waits for them, and re-layouts: 3.38 us -> 1.42 us
  Pallas kernels: 19.5 us -> 18.9 us
    unnamed x2, local copies, waits for them, and re-layouts: 3.38 us -> 1.42 us
    pallas_call x1, Pallas kernels: 19.5 us -> 18.9 us  [local(): pl.pallas_call(functools.partial(kernel, sizes), out_shape=(pltpu.VMEM((n...]
where the time goes in v3:
time: 21.1 us; the launch traced here: 20.9 us
  Pallas kernels  18.9 us (90%)
  local copies, waits for them, and re-layouts  1.42 us (7%)
  between operations  0.64 us (3%)
    pallas_call x1, Pallas kernels, local(): pl.pallas_call(functools.partial(kernel, sizes), out_shape=(pltpu.VMEM((n...  18.9 us
    unnamed x2, local copies, waits for them, and re-layouts  1.42 us

profile of v3, /device:TPU:1, one launch (start us, length us, event | category | flops | bytes accessed | tf_op | source)
XLA Modules:
  0.0 20.9 jit_solution(9411675012968910021)
XLA Ops:
  0.6 18.9 %shard_map.77 = (f32[8,48,256]{2,1,0:T(8,128)S(1)}, f32[3,64,256]{2,1,0:T(8,128)S(1)}) custom-call(f32[3,8,48,256]{3,2,1,0:T(8,128)} %near.1, s32[1,1,512]{2,1,0:T(1,128)} %bitcast.1, s32[1,1,512]{2,1,0:T(1,128)} %land_in.1, f32[64,256]{1,0:T(8,128)} %dep_in.1, f32[2,64,256]{2,1,0:T(8,128)} %flow_in.1, s32[64,256]{1,0:T(8,128)} %wet_in.1), custom_call_target="tpu_custom_call" | custom-call | tf_op jit(solution)/shard_map/pallas_call | solution.py:323
  19.5 0.7 %copy.10 = f32[8,48,256]{2,1,0:T(8,128)} copy(f32[8,48,256]{2,1,0:T(8,128)S(1)} %get-tuple-element.2) | data formatting | bytes 786432
  20.3 0.7 %copy.11 = f32[3,64,256]{2,1,0:T(8,128)} copy(f32[3,64,256]{2,1,0:T(8,128)S(1)} %get-tuple-element.3) | data formatting | bytes 393216
